TPU v7x, 256 devices: a whole 4x4x8 slice. The times are simulated.
256 devices in a mesh: section: 2 (over z_hi), dp: 8 (over x, core), tensor: 16 (over y, z_lo).
Axes of the slice: x: 4, y: 4, z: 8 (z_hi: 2, z_lo: 4; z = z_hi * 4 + z_lo), core: 2. Of those that a mesh axis runs over, the one named last changes fastest.
Arguments:
- hidden: bfloat16 [256, 16384], P('dp'), may hold values from -6 to 6
- query_weight: bfloat16 [2, 16384, 16384], P('section', 'dp', 'tensor'), may hold values from -0.046875 to 0.046875
- out_weight: bfloat16 [2, 16384, 16384], P('section', 'tensor', 'dp'), may hold values from -0.28125 to 0.28125
- key_cache: bfloat16 [2, 256, 256, 1024], P('section', 'dp', None, 'tensor'), may hold values from -400 to 400
- value_cache: bfloat16 [2, 256, 256, 1024], P('section', 'dp', None, 'tensor'), may hold values from -6 to 6
- cache_lengths: int32 [256], P('dp'), may hold values from 32 to 256, as said below
Outputs:
- layer_outputs: bfloat16 [2, 256, 16384], P('section', 'dp')
Inputs may be any that keep to these rules, and one draw needn't show every extreme that they name: `cache_lengths`: in every aligned block of 32 rows some row has all 256 positions live.
All inputs are finite; a program needn't handle non-finite values.
Results may differ from a plain program's by a relative error of at most 0.01595.
Values may be sent and summed in bfloat16 or wider, within the bound.
No kernel may reach another device: no remote copies, remote signals or barrier semaphores. Data moves between devices by JAX's collectives and lax.ppermute only.
A program may use at most 64 MiB of HBM per device.

v0:
```python
import math

import jax
import jax.numpy as jnp
from jax import lax
from jax.sharding import PartitionSpec as P


def swapped(shard, axis, apart):
    return lax.ppermute(shard, axis, [(i, i ^ 1 << apart) for i in range(lax.axis_size(axis))])


def shifted(block, axis, distance):
    devices = range(lax.axis_size(axis))
    route = [(i - distance, i) for i in devices if i - distance in devices]
    return lax.ppermute(block, axis, route)


def spread_back(share):
    span = lax.all_gather(share, "tensor", axis=1, tiled=True)
    spread = lax.all_to_all(span, "dp", split_axis=0, concat_axis=1, tiled=True)
    return spread.astype(jnp.float32)


def layer_step(state, query_part, out_part, key_half, value_half, row_lengths):
    rows_here, model_width = state.shape
    head_size = 2 * key_half.shape[-1]
    cache_len = key_half.shape[1]
    wide_rows = state.astype(jnp.float32)
    normed = (
        wide_rows * lax.rsqrt(jnp.mean(wide_rows * wide_rows, axis=-1, keepdims=True) + 1e-05)
    ).astype(jnp.bfloat16)
    normed_cols = lax.all_to_all(normed, "dp", split_axis=1, concat_axis=0, tiled=True)
    queries = lax.psum_scatter(
        jnp.dot(normed_cols, query_part, preferred_element_type=jnp.float32),
        "dp",
        scatter_dimension=0,
        tiled=True,
    ).astype(jnp.bfloat16)
    head_count = queries.shape[1] // head_size
    queries = queries.reshape(rows_here, head_count, head_size)
    partner_key, partner_value = swapped((key_half, value_half), "tensor", 0)
    is_odd = lax.axis_index("tensor") % 2 == 1
    key_rows = jnp.concatenate(
        [jnp.where(is_odd, partner_key, key_half), jnp.where(is_odd, key_half, partner_key)],
        axis=-1,
    )
    value_rows = jnp.concatenate(
        [
            jnp.where(is_odd, partner_value, value_half),
            jnp.where(is_odd, value_half, partner_value),
        ],
        axis=-1,
    )
    scores = jnp.einsum(
        "rnh,rlh->rnl", queries, key_rows, preferred_element_type=jnp.float32
    ) / math.sqrt(head_size)
    live_mask = (jnp.arange(cache_len, dtype=jnp.int32)[None, :] < row_lengths[:, None])[:, None, :]
    scores = jnp.where(live_mask, scores, -1e30)
    row_max = jnp.max(scores, axis=-1, keepdims=True)
    expd = jnp.where(live_mask, jnp.exp(scores - row_max), 0.0)
    weights_bf = (expd / jnp.sum(expd, axis=-1, keepdims=True)).astype(jnp.bfloat16)
    attended = jnp.einsum(
        "rnl,rlh->rnh", weights_bf, value_rows, preferred_element_type=jnp.float32
    ).astype(jnp.bfloat16)
    attended = attended.reshape(rows_here, head_count * head_size)
    partial_value = jnp.dot(
        lax.all_gather(attended, "dp", axis=0, tiled=True),
        out_part,
        preferred_element_type=jnp.float32,
    ).astype(jnp.bfloat16)
    received = lax.all_to_all(
        partial_value[None], "tensor", split_axis=2, concat_axis=0, tiled=True
    )
    share = jnp.sum(received.astype(jnp.float32), axis=0).astype(jnp.bfloat16)
    return (wide_rows, share)


def body(hidden, query_weight, out_weight, key_cache, value_cache, cache_lengths):
    sections = lax.axis_size("section")
    section_id = lax.axis_index("section")
    inputs = hidden
    result = jnp.zeros_like(hidden)
    for moment in range(sections):
        wide_rows, share = layer_step(
            inputs, query_weight[0], out_weight[0], key_cache[0], value_cache[0], cache_lengths
        )
        updated = (wide_rows + spread_back(share)).astype(jnp.bfloat16)
        result = jnp.where(section_id == moment, updated, result)
        if moment + 1 < sections:
            arrived = shifted(updated, "section", 1)
            inputs = jnp.where(section_id == 0, hidden, arrived)
    return result[None]


def solution(mesh):
    in_specs = (
        P("dp", None),
        P("section", "dp", "tensor"),
        P("section", "tensor", "dp"),
        P("section", "dp", None, "tensor"),
        P("section", "dp", None, "tensor"),
        P("dp"),
    )
    out_specs = P("section", "dp", None)
    return jax.shard_map(body, mesh=mesh, in_specs=in_specs, out_specs=out_specs, check_vma=False)
```

profile of v0, /device:TPU:1, one launch (start us, length us, event | category | flops | bytes accessed | tf_op | source)
XLA Modules:
  0.0 560.9 jit_solution(6045964445467655310)
XLA Ops:
  9.7 21.0 %all_to_all.88 = bf16[32,8,2048]{2,0,1:T(8,128)(2,1)S(1)} all-to-all(bf16[32,8,2048]{2,0,1:T(8,128)(2,1)S(1)} %bitcast.92), channel_id=1, replica_groups=mesh['section'=2,'dp'=8,'tensor'=16] {'dp'}, dimensions={1} | all-to-all | bytes 2097152 | tf_op jit(solution)/shard_map/all_to_all | solution.py:33
  38.4 18.6 %collective-permute-done.1 = bf16[32,256,64]{1,2,0:T(8,128)(2,1)} collective-permute-done((bf16[32,256,64]{1,2,0:T(8,128)(2,1)S(1)}, bf16[32,256,64]{1,2,0:T(8,128)(2,1)}, u32[]{:S(2)}, u32[]{:S(2)}) %collective-permute-start.1) | collective-permute-done | bytes 1048608 | tf_op jit(solution)/shard_map/ppermute | solution.py:10
  59.8 19.6 %collective-permute-done = bf16[32,256,64]{1,2,0:T(8,128)(2,1)S(1)} collective-permute-done((bf16[32,256,64]{1,2,0:T(8,128)(2,1)S(1)}, bf16[32,256,64]{1,2,0:T(8,128)(2,1)S(1)}, u32[]{:S(2)}, u32[]{:S(2)}) %collective-permute-start) | collective-permute-done | bytes 1048608 | tf_op jit(solution)/shard_map/ppermute | solution.py:10
  81.2 4.0 bitcast_select_fusion.2
  88.3 3.0 fusion.54
  91.3 3.6 convolution_convert_fusion.1
  94.9 15.0 %all_gather.12 = bf16[256,1024]{1,0:T(8,128)(2,1)S(1)} all-gather(bf16[32,1024]{1,0:T(8,128)(2,1)S(1)} %bitcast.103), channel_id=1, replica_groups=mesh['section'=2,'dp'=8,'tensor'=16] {'dp'}, dimensions={0}, use_global_device_ids=true | all-gather | bytes 589824 | tf_op jit(solution)/shard_map/all_gather | solution.py:68
  111.2 3.8 copy.54
  115.5 11.7 %reduce.8 = bf16[2048,256]{1,0:T(8,128)(2,1)S(1)} reduce(bf16[2048,1,256]{2,1,0:T(2,128)(2,1)} %bitcast.85, bf16[]{:T(256)} %broadcast.68), dimensions={1}, to_apply=%bitcast.68.reduce_sub_computation | reduce | bytes 2097154
  128.3 35.3 %all_to_all.89 = bf16[16,2,16384]{2,1,0:T(2,128)(2,1)S(1)} all-to-all(bf16[16,2,16384]{2,1,0:T(2,128)(2,1)} %reshape.73), channel_id=1, replica_groups=mesh['section'=2,'dp'=8,'tensor'=16] {'tensor'}, dimensions={0} | all-to-all | bytes 2097152 | tf_op jit(solution)/shard_map/all_to_all | solution.py:72
  163.6 3.5 reshape.74
  169.7 69.7 %all-gather.3.cloned.1.call-done = bf16[256,2048]{0,1:T(8,128)(2,1)} async-done(((bf16[256,128]{0,1:T(8,128)(2,1)}), bf16[256,2048]{0,1:T(8,128)(2,1)}) %all-gather.3.cloned.1.call-update) | async-done | bytes 1048592 | tf_op jit(solution)/shard_map/all_gather | solution.py:20
  240.9 29.4 %all_to_all.90 = bf16[8,32,2048]{2,1,0:T(8,128)(2,1)S(1)} all-to-all(bf16[8,32,2048]{2,1,0:T(8,128)(2,1)S(1)} %bitcast.93), channel_id=1, replica_groups=mesh['section'=2,'dp'=8,'tensor'=16] {'dp'}, dimensions={0} | all-to-all | bytes 2097152 | tf_op jit(solution)/shard_map/all_to_all | solution.py:21
  273.0 8.0 %collective-permute-start.2 = (bf16[32,16384]{1,0:T(8,128)(2,1)}, bf16[32,16384]{1,0:T(8,128)(2,1)}, u32[]{:S(2)}, u32[]{:S(2)}) collective-permute-start(bf16[32,16384]{1,0:T(8,128)(2,1)} %fusion.24), channel_id=1, source_target_pairs={{0,128},{1,129},{2,130},{3,131},{4,132},{5,133},{6,134},{7,135},{8... | collective-permute-start | bytes 3145736 | tf_op jit(solution)/shard_map/ppermute | solution.py:16
  281.1 20.7 %collective-permute-done.2 = bf16[32,16384]{1,0:T(8,128)(2,1)} collective-permute-done((bf16[32,16384]{1,0:T(8,128)(2,1)}, bf16[32,16384]{1,0:T(8,128)(2,1)}, u32[]{:S(2)}, u32[]{:S(2)}) %collective-permute-start.2) | collective-permute-done | bytes 1048608 | tf_op jit(solution)/shard_map/ppermute | solution.py:16
  303.3 19.6 %all_to_all.91 = bf16[32,8,2048]{2,0,1:T(8,128)(2,1)S(1)} all-to-all(bf16[32,8,2048]{2,0,1:T(8,128)(2,1)S(1)} %bitcast.94), channel_id=1, replica_groups=mesh['section'=2,'dp'=8,'tensor'=16] {'dp'}, dimensions={1} | all-to-all | bytes 2097152 | tf_op jit(solution)/shard_map/all_to_all | solution.py:33
  325.2 51.1 %reduce-scatter.5.cloned.1.call-done = f32[32,1024]{1,0:T(8,128)} async-done(((f32[256,1024]{1,0:T(8,128)}), f32[32,1024]{1,0:T(8,128)}) %reduce-scatter.5.cloned.1.call-update) | async-done | bytes 131088 | tf_op jit(solution)/shard_map/reduce_scatter | solution.py:34
  380.3 3.6 convolution_convert_fusion
  383.9 16.1 %all_gather.14 = bf16[256,1024]{1,0:T(8,128)(2,1)S(1)} all-gather(bf16[32,1024]{1,0:T(8,128)(2,1)S(1)} %bitcast.104), channel_id=1, replica_groups=mesh['section'=2,'dp'=8,'tensor'=16] {'dp'}, dimensions={0}, use_global_device_ids=true | all-gather | bytes 589824 | tf_op jit(solution)/shard_map/all_gather | solution.py:68
  403.0 10.6 %reduce.9 = bf16[2048,256]{1,0:T(8,128)(2,1)S(1)} reduce(bf16[2048,1,256]{2,1,0:T(2,128)(2,1)S(1)} %bitcast.86, bf16[]{:T(256)} %broadcast.68), dimensions={1}, to_apply=%bitcast.70.reduce_sub_computation | reduce | bytes 2097154
  413.9 34.0 %all_to_all.92 = bf16[16,2,16384]{2,1,0:T(2,128)(2,1)S(1)} all-to-all(bf16[16,2,16384]{2,1,0:T(2,128)(2,1)S(1)} %reshape.75), channel_id=1, replica_groups=mesh['section'=2,'dp'=8,'tensor'=16] {'tensor'}, dimensions={0} | all-to-all | bytes 2097152 | tf_op jit(solution)/shard_map/all_to_all | solution.py:72
  450.0 68.3 %all-gather.5.cloned.1.call-done = bf16[256,2048]{0,1:T(8,128)(2,1)} async-done(((bf16[256,128]{0,1:T(8,128)(2,1)}), bf16[256,2048]{0,1:T(8,128)(2,1)}) %all-gather.5.cloned.1.call-update) | async-done | bytes 1048592 | tf_op jit(solution)/shard_map/all_gather | solution.py:20
  520.6 14.6 %all-to-all-start.5 = ((bf16[8,32,2048]{2,1,0:T(8,128)(2,1)}), bf16[8,32,2048]{2,1,0:T(8,128)(2,1)S(1)}, u32[]{:S(2)}, u32[]{:S(2)}) async-start(bf16[8,32,2048]{2,1,0:T(8,128)(2,1)} %bitcast.14), calls=%async_computation.7 | async-start | bytes 2097152 | tf_op jit(solution)/shard_map/all_to_all | solution.py:21
  535.1 15.1 %all-to-all-done.5 = bf16[8,32,2048]{2,1,0:T(8,128)(2,1)S(1)} async-done(((bf16[8,32,2048]{2,1,0:T(8,128)(2,1)}), bf16[8,32,2048]{2,1,0:T(8,128)(2,1)S(1)}, u32[]{:S(2)}, u32[]{:S(2)}) %all-to-all-start.5) | async-done | bytes 1048608 | tf_op jit(solution)/shard_map/all_to_all | solution.py:21
  (77 shorter events, 47.5 us)
Async XLA Ops:
  6.5 80.8 %reduce-scatter.3.cloned.1.call-start = ((), (), s32[]{:S(2)}) async-start(), calls=%async_computation.8 | async-start | bytes 1179648 | tf_op jit(solution)/shard_map/reduce_scatter | solution.py:34
  9.6 21.1 %copy-start.8 = (bf16[1,2048,1024]{2,1,0:T(8,128)(2,1)S(1)}, bf16[1,2048,1024]{2,1,0:T(8,128)(2,1)}, u32[]{:S(2)}) copy-start(bf16[1,2048,1024]{2,1,0:T(8,128)(2,1)} %param.7) | copy-start | bytes 12582916
  30.7 2.3 copy-start.5
  30.7 4.0 copy-start.6
  32.9 206.5 %all-gather.3.cloned.1.call-start = ((), (), s32[]{:S(2)}) async-start(), calls=%async_computation.9 | async-start | bytes 1114112 | tf_op jit(solution)/shard_map/all_gather | solution.py:20
  33.0 24.1 %collective-permute-start.1 = (bf16[32,256,64]{1,2,0:T(8,128)(2,1)S(1)}, bf16[32,256,64]{1,2,0:T(8,128)(2,1)}, u32[]{:S(2)}, u32[]{:S(2)}) collective-permute-start(bf16[32,256,64]{1,2,0:T(8,128)(2,1)S(1)} %bitcast.95), channel_id=1, source_target_pairs={{0,1},{1,0},{2,3},{3,2},{4,5},{5,4},{6,7},{7,6},{8,9},{9,8},{10,11... | collective-permute-start | bytes 3145736 | tf_op jit(solution)/shard_map/ppermute | solution.py:10
  34.6 44.8 %collective-permute-start = (bf16[32,256,64]{1,2,0:T(8,128)(2,1)S(1)}, bf16[32,256,64]{1,2,0:T(8,128)(2,1)S(1)}, u32[]{:S(2)}, u32[]{:S(2)}) collective-permute-start(bf16[32,256,64]{1,2,0:T(8,128)(2,1)S(1)} %bitcast.96), channel_id=1, source_target_pairs={{0,1},{1,0},{2,3},{3,2},{4,5},{5,4},{6,7},{7,6},{8,9},{9,8},{10,11... | collective-permute-start | bytes 3145736 | tf_op jit(solution)/shard_map/ppermute | solution.py:10
  36.6 1.8 copy-start.7
  81.2 4.0 copy-start.3
  81.2 4.0 copy-start.4
  91.3 18.6 %copy-start.10 = (bf16[1,1024,2048]{2,1,0:T(8,128)(2,1)S(1)}, bf16[1,1024,2048]{2,1,0:T(8,128)(2,1)}, u32[]{:S(2)}) copy-start(bf16[1,1024,2048]{2,1,0:T(8,128)(2,1)} %param.8) | copy-start | bytes 12582916
  169.6 206.7 %reduce-scatter.5.cloned.1.call-start = ((), (), s32[]{:S(2)}) async-start(), calls=%async_computation.10 | async-start | bytes 1179648 | tf_op jit(solution)/shard_map/reduce_scatter | solution.py:34
  270.6 1.2 copy-start
  273.0 28.8 %collective-permute-start.2 = (bf16[32,16384]{1,0:T(8,128)(2,1)}, bf16[32,16384]{1,0:T(8,128)(2,1)}, u32[]{:S(2)}, u32[]{:S(2)}) collective-permute-start(bf16[32,16384]{1,0:T(8,128)(2,1)} %fusion.24), channel_id=1, source_target_pairs={{0,128},{1,129},{2,130},{3,131},{4,132},{5,133},{6,134},{7,135},{8... | collective-permute-start | bytes 3145736 | tf_op jit(solution)/shard_map/ppermute | solution.py:16
  302.3 1.0 copy-start.1
  302.5 20.3 %copy-start.9 = (bf16[1,2048,1024]{2,1,0:T(8,128)(2,1)S(1)}, bf16[1,2048,1024]{2,1,0:T(8,128)(2,1)}, u32[]{:S(2)}) copy-start(bf16[1,2048,1024]{2,1,0:T(8,128)(2,1)} %param.7) | copy-start | bytes 12582916
  325.2 193.1 %all-gather.5.cloned.1.call-start = ((), (), s32[]{:S(2)}) async-start(), calls=%async_computation.11 | async-start | bytes 1114112 | tf_op jit(solution)/shard_map/all_gather | solution.py:20
  380.3 19.7 %copy-start.11 = (bf16[1,1024,2048]{2,1,0:T(8,128)(2,1)S(1)}, bf16[1,1024,2048]{2,1,0:T(8,128)(2,1)}, u32[]{:S(2)}) copy-start(bf16[1,1024,2048]{2,1,0:T(8,128)(2,1)} %param.8) | copy-start | bytes 12582916
  520.6 29.7 %all-to-all-start.5 = ((bf16[8,32,2048]{2,1,0:T(8,128)(2,1)}), bf16[8,32,2048]{2,1,0:T(8,128)(2,1)S(1)}, u32[]{:S(2)}, u32[]{:S(2)}) async-start(bf16[8,32,2048]{2,1,0:T(8,128)(2,1)} %bitcast.14), calls=%async_computation.7 | async-start | bytes 2097152 | tf_op jit(solution)/shard_map/all_to_all | solution.py:21
  550.5 1.2 copy-start.2
Sparse Core Ops, SparseCore 0:
  33.0 33.4 reduce-scatter.2
  169.8 69.6 all-gather.2
  325.3 51.0 reduce-scatter.4
  450.1 68.1 all-gather.4
where the time goes:
time: 562 us; the launch traced here: 561 us
  waiting for transfers between devices  263 us (47%)
  blocking collectives  170 us (30%)
  other arithmetic  39.9 us (7%)
  local copies, waits for them, and re-layouts  29.1 us (5%)
  starting transfers between devices  24.5 us (4%)
  matrix products  20.3 us (4%)
  between operations  13.4 us (2%)
    all_gather x2, waiting for transfers between devices, spread_back(): span = lax.all_gather(share, 'tensor', axis=1, tiled=True)  138 us
    all_to_all x2, blocking collectives, layer_step(): lax.all_to_all(partial_value[None], 'tensor', split_axis=2, concat_axis=0...  69.3 us
    reduce_scatter x2, waiting for transfers between devices, layer_step(): lax.psum_scatter(jnp.dot(normed_cols, query_part, preferred_element_type=...  51.2 us
    all_to_all x2, blocking collectives, layer_step(): lax.all_to_all(normed, 'dp', split_axis=1, concat_axis=0, tiled=True)  40.5 us
    ppermute x2, waiting for transfers between devices, swapped(): lax.ppermute(shard, axis, [(i, i ^ 1 << apart) for i in range(lax.axis_si...  38.2 us
    all_gather x2, blocking collectives, layer_step(): lax.all_gather(attended, 'dp', axis=0, tiled=True)  31.1 us
    all_to_all x1, blocking collectives, spread_back(): spread = lax.all_to_all(span, 'dp', split_axis=0, concat_axis=1, tiled=True)  29.4 us
    unnamed x6, other arithmetic  24.6 us
  transfers between devices with their start and end apart: 8, of which 7 were waited for; matrix products, arithmetic and copies ran while one was open for 3% of the time, Pallas kernels for 0%

commit v1 on v0

v1 whole, which is shorter than its diff:
```python
import jax
import jax.numpy as jnp
from jax import lax
from jax.experimental import pallas as pl
from jax.experimental.pallas import tpu as pltpu
from jax.sharding import Mesh, PartitionSpec as P

DP = ("x", "c")
DEPTH = ("zh", "zl")
TENSOR = ("y", "zh", "zl")
PAIRED = ("x", "c", "zl")
BF = jnp.bfloat16
F32 = jnp.float32
VMEM = pl.BlockSpec(memory_space=pltpu.VMEM)
SMEM = pl.BlockSpec(memory_space=pltpu.SMEM)
LIMIT = 48 * 1024 * 1024


def call(kernel, out_shapes, in_specs, args, flops=0, name=None):
    single = not isinstance(out_shapes, (list, tuple))
    shapes = [out_shapes] if single else list(out_shapes)
    moved = sum(a.size * a.dtype.itemsize for a in list(args) + shapes)
    return pl.pallas_call(
        kernel,
        out_shape=out_shapes,
        in_specs=in_specs,
        out_specs=VMEM if single else [VMEM] * len(shapes),
        compiler_params=pltpu.CompilerParams(vmem_limit_bytes=LIMIT),
        cost_estimate=pl.CostEstimate(flops=flops, bytes_accessed=moved, transcendentals=0),
        name=name,
    )(*args)


def gathered(block, axes):
    count = lax.axis_size(axes)
    return [block] + [
        lax.ppermute(block, axes, [(i, (i + k) % count) for i in range(count)])
        for k in range(1, count)
    ]


def traded(blocks, axes):
    return lax.all_to_all(blocks, axes, split_axis=0, concat_axis=0, tiled=True)


def project(columns, weight_ref, out_ref):
    rows, depth = columns.shape
    width = weight_ref.shape[1]
    wide = columns[...].astype(F32)
    squares = jnp.sum(wide * wide, axis=1, keepdims=True)
    high = squares.astype(BF)
    rest = squares - high.astype(F32)
    middle = rest.astype(BF)
    low = (rest - middle.astype(F32)).astype(BF)
    lane = lax.broadcasted_iota(jnp.int32, (rows, 128), 1)
    out_ref[:, width:] = jnp.where(
        lane == 0,
        high.astype(F32),
        jnp.where(lane == 1, middle.astype(F32), jnp.where(lane == 2, low.astype(F32), 0.0)),
    ).astype(BF)

    @pl.loop(0, width // 256)
    def _(tile):
        span = pl.ds(pl.multiple_of(tile * 256, 256), 256)
        out_ref[:, span] = jnp.dot(
            columns[...], weight_ref[:, span], preferred_element_type=F32
        ).astype(BF)


def project_whole(columns_ref, weight_ref, out_ref):
    project(columns_ref, weight_ref, out_ref)


def project_chunks(place_ref, own_ref, one_ref, two_ref, three_ref, weight_ref, out_ref, held):
    y, z = place_ref[0], place_ref[1]
    for step, source in enumerate((own_ref, one_ref, two_ref, three_ref)):
        for depth in range(source.shape[0]):
            index = lax.rem(y - step + 4, 4) * 4 + lax.rem(z - depth + 4, 4)
            held[:, pl.ds(pl.multiple_of(index * 128, 128), 128)] = source[depth]
    project(held, weight_ref, out_ref)


def attend(place_ref, sums_ref, live_ref, key_ref, key_other_ref, value_ref, value_other_ref, out_ref):
    half = place_ref[2]
    rows = sums_ref.shape[1]
    width = sums_ref.shape[2] - 128
    sources = sums_ref.shape[0] // 2
    heads = []
    for part in range(2):
        total = sums_ref[part].astype(F32)
        for source in range(1, sources):
            total += sums_ref[2 * source + part].astype(F32)
        squares = total[:, width : width + 1] + total[:, width + 1 : width + 2]
        squares = squares + total[:, width + 2 : width + 3]
        scale = lax.rsqrt(squares / 16384.0 + 1e-05)
        scaled = total[:, :width] * scale
        heads += [scaled[:, h * 128 : (h + 1) * 128] for h in range(width // 128)]
    queries = jnp.concatenate(heads, axis=0)
    count = queries.shape[0]
    turned = pltpu.roll(queries, 64, 1)
    lane = lax.broadcasted_iota(jnp.int32, (count, 128), 1)
    row = lax.rem(lax.broadcasted_iota(jnp.int32, (count, 128), 0), rows)
    first = lane < 64
    low = jnp.where(first, queries, turned)
    high = jnp.where(first, turned, queries)
    is_low = half == 0
    own_q = jnp.where(is_low, low, high)
    other_q = jnp.where(is_low, high, low)

    def spread(block):
        return jnp.concatenate(
            [
                jnp.where(row == 2 * k + jnp.where(first, 0, 1), block, 0.0).astype(BF)
                for k in range(rows // 2)
            ],
            axis=1,
        )

    mine = pl.ds(half * rows, rows)
    depth = key_ref.shape[1]
    cache_len = key_ref.shape[2]
    own_key = key_ref[mine].reshape(rows * depth, cache_len)
    other_key = key_other_ref[...].reshape(rows * depth, cache_len)
    scores = jnp.dot(spread(own_q), own_key, preferred_element_type=F32)
    scores += jnp.dot(spread(other_q), other_key, preferred_element_type=F32)
    scores = scores * (128.0**-0.5)
    position = lax.broadcasted_iota(jnp.int32, scores.shape, 1)
    live = position < live_ref[...]
    scores = jnp.where(live, scores, -1e30)
    top = jnp.max(scores, axis=1, keepdims=True)
    expd = jnp.where(live, jnp.exp(scores - top), 0.0)
    probs = (expd / jnp.sum(expd, axis=1, keepdims=True)).astype(BF)

    def blend(values):
        flat = values.reshape(rows * depth, cache_len)
        product = lax.dot_general(
            probs, flat, (((1,), (1,)), ((), ())), preferred_element_type=F32
        )
        total = jnp.zeros((count, 128), F32)
        for k in range(rows // 2):
            total += jnp.where(row // 2 == k, product[:, k * 128 : (k + 1) * 128], 0.0)
        return total

    own = blend(value_ref[mine])
    other = blend(value_other_ref[...])
    odd = lax.rem(row, 2)
    own = jnp.where(odd == half, own, pltpu.roll(own, 64, 1))
    other = jnp.where(odd == half, pltpu.roll(other, 64, 1), other)
    attended = jnp.where(jnp.where(first, 0, 1) == half, own, other).astype(BF)
    for part in range(2):
        for h in range(width // 128):
            start = (part * (width // 128) + h) * rows
            tile = attended[start : start + rows]
            for target in range(sources):
                out_ref[2 * target + part, :, h * 128 : (h + 1) * 128] = tile


def emit(rows_ref, weight_ref, out_ref):
    tiles = out_ref.shape[0] // 2

    @pl.loop(0, tiles)
    def _(tile):
        span = pl.ds(pl.multiple_of(tile * 256, 256), 256)
        product = jnp.dot(rows_ref[...], weight_ref[:, span], preferred_element_type=F32).astype(BF)
        out_ref[2 * tile] = product[:, :128]
        out_ref[2 * tile + 1] = product[:, 128:]


def merge(blocks_ref, out_ref):
    total = blocks_ref[0].astype(F32)
    for source in range(1, blocks_ref.shape[0]):
        total += blocks_ref[source].astype(F32)
    out_ref[...] = total.astype(BF)


def merge_state(blocks_ref, state_ref, out_ref):
    total = blocks_ref[0].astype(F32)
    for source in range(1, blocks_ref.shape[0]):
        total += blocks_ref[source].astype(F32)
    total = total.astype(BF).astype(F32)
    out_ref[...] = (state_ref[...].astype(F32) + total).astype(BF)


def lay_out(place_ref, own_ref, one_ref, two_ref, three_ref, out_ref):
    y, z = place_ref[0], place_ref[1]
    for step, source in enumerate((own_ref, one_ref, two_ref, three_ref)):
        for depth in range(4):
            index = lax.rem(y - step + 4, 4) * 4 + lax.rem(z - depth + 4, 4)
            for part in range(8):
                start = pl.multiple_of(index * 128 + part * 2048, 128)
                out_ref[:, pl.ds(start, 128)] = source[depth, part]


def layer(partial, state, place, live, out_weight, key, key_other, value, value_other):
    rows, wide = partial.shape
    sums = traded(partial.reshape(16, rows // 16, wide), PAIRED)
    sent = call(
        attend,
        jax.ShapeDtypeStruct((16, rows // 16, wide - 128), BF),
        [SMEM] + [VMEM] * 6,
        (place, sums, live, key, key_other, value, value_other),
        flops=4 * rows * 2048 * 256,
        name="attend",
    )
    attended = traded(sent, PAIRED).reshape(rows, wide - 128)
    blocks = call(
        emit,
        jax.ShapeDtypeStruct((16, rows, 128), BF),
        [VMEM, VMEM],
        (attended, out_weight),
        flops=2 * rows * 1024 * 2048,
        name="emit",
    )
    blocks = traded(blocks.reshape(4, 4, rows, 128), "y")
    blocks = call(merge, jax.ShapeDtypeStruct((4, rows, 128), BF), [VMEM], (blocks,), name="merge")
    blocks = traded(blocks, DEPTH)
    return call(
        merge_state,
        jax.ShapeDtypeStruct((rows, 128), BF),
        [VMEM, VMEM],
        (blocks, state),
        name="merge_state",
    )


def body(hidden, query_weight, out_weight, key_cache, value_cache, cache_lengths):
    y = lax.axis_index("y")
    z = lax.axis_index(DEPTH)
    half = lax.axis_index("zl")
    place = jnp.stack([y, z, half]).astype(jnp.int32)
    query_weight, out_weight = query_weight[0], out_weight[0]
    key = jnp.swapaxes(key_cache[0], 1, 2)
    value = jnp.swapaxes(value_cache[0], 1, 2)
    swap = [(0, 1), (1, 0)]
    far = (1 - half) * 16
    key_other = lax.ppermute(lax.dynamic_slice_in_dim(key, far, 16, 0), "zl", swap)
    value_other = lax.ppermute(lax.dynamic_slice_in_dim(value, far, 16, 0), "zl", swap)
    lengths = lax.dynamic_slice_in_dim(cache_lengths, half * 16, 16, 0)
    live = jnp.tile(lengths, 16)[:, None]

    rows_here, wide = hidden.shape
    columns = traded(jnp.swapaxes(hidden.reshape(rows_here, 8, wide // 8), 0, 1), DP)
    columns = columns.reshape(8 * rows_here, wide // 8)
    rows = columns.shape[0]
    state = lax.dynamic_slice_in_dim(columns, (y * 4 + z) * 128, 128, 1)
    partial_shape = jax.ShapeDtypeStruct((rows, query_weight.shape[1] + 128), BF)
    flops = 2 * rows * query_weight.shape[0] * query_weight.shape[1]
    partial = call(
        project_whole, partial_shape, [VMEM, VMEM], (columns, query_weight), flops, "project"
    )
    caches = (out_weight, key, key_other, value, value_other)
    first = layer(partial, state, place, live, *caches)

    arrived = lax.ppermute(first, "s", [(0, 1)])
    chunks = gathered(jnp.stack(gathered(arrived, DEPTH)), "y")
    partial = pl.pallas_call(
        project_chunks,
        out_shape=partial_shape,
        in_specs=[SMEM] + [VMEM] * 5,
        out_specs=VMEM,
        scratch_shapes=[pltpu.VMEM((rows, wide // 8), BF)],
        compiler_params=pltpu.CompilerParams(vmem_limit_bytes=LIMIT),
        cost_estimate=pl.CostEstimate(flops=flops, bytes_accessed=6 << 20, transcendentals=0),
        name="project_chunks",
    )(place, *chunks, query_weight)
    second = layer(partial, arrived, place, live, *caches)

    result = jnp.where(lax.axis_index("s") == 0, first, second)
    result = traded(result.reshape(8, rows_here, 128), DP)
    pieces = gathered(jnp.stack(gathered(result, DEPTH)), "y")
    out = call(
        lay_out,
        jax.ShapeDtypeStruct((rows_here, wide), BF),
        [SMEM] + [VMEM] * 4,
        (place, *pieces),
        name="lay_out",
    )
    return out[None]


def solution(mesh):
    fine = Mesh(mesh.devices.reshape(2, 4, 2, 4, 2, 2), ("s", "x", "c", "y", "zh", "zl"))
    in_specs = (
        P(DP, None),
        P("s", DP, TENSOR),
        P("s", TENSOR, DP),
        P("s", DP, None, TENSOR),
        P("s", DP, None, TENSOR),
        P(DP),
    )
    out_specs = P("s", DP, None)
    return jax.shard_map(body, mesh=fine, in_specs=in_specs, out_specs=out_specs, check_vma=False)
```

time: 562 us -> 252 us (0.45)
  waiting for transfers between devices: 263 us -> 76.1 us
  blocking collectives: 170 us -> 115 us
  other arithmetic: 39.9 us -> 0.16 us
  local copies, waits for them, and re-layouts: 29.1 us -> 7.84 us
  matrix products: 20.3 us -> 0 us
  Pallas kernels: 0 us -> 20.2 us
  between operations: 13.4 us -> 0.17 us
  starting transfers between devices: 24.5 us -> 31.6 us
    all_gather x2 -> x0, waiting for transfers between devices: 138 us -> none  [spread_back(): span = lax.all_gather(share, 'tensor', axis=1, tiled=True)]
    reduce_scatter x2 -> x0, waiting for transfers between devices: 51.2 us -> none  [layer_step(): lax.psum_scatter(jnp.dot(normed_cols, query_part, preferred_element_type=...]
    all_gather x2 -> x0, blocking collectives: 31.1 us -> none  [layer_step(): lax.all_gather(attended, 'dp', axis=0, tiled=True)]
    unnamed x6 -> x0, other arithmetic: 24.6 us -> none
    all_to_all x5 -> x7, blocking collectives: 139 us -> 115 us  [traded(): return lax.all_to_all(blocks, axes, split_axis=0, concat_axis=0, tiled=True)]
    pallas_call x0 -> x11, Pallas kernels: none -> 20.2 us  [the longest x10 17.2 us: call(): pl.pallas_call(kernel, out_shape=out_shapes, in_specs=in_specs, out_specs...]
    dot_general x6 -> x0, matrix products: 14.3 us -> none  [the longest x2 7.2 us: layer_step(): jnp.einsum('rnl,rlh->rnh', weights_bf, value_rows, preferred_element_type...]
    unnamed x37 -> x18, local copies, waits for them, and re-layouts: 14.7 us -> 3.86 us
  transfers between devices with their start and end apart: 8 -> 18, of which waited for: 7 -> 16; matrix products, arithmetic and copies ran while one was open for 3% -> 1% of each run, Pallas kernels for 0% -> 0%
where the time goes in v1:
time: 252 us; the launch traced here: 251 us
  blocking collectives  115 us (46%)
  waiting for transfers between devices  76.1 us (30%)
  starting transfers between devices  31.6 us (13%)
  Pallas kernels  20.2 us (8%)
  local copies, waits for them, and re-layouts  7.84 us (3%)
    all_to_all x7, blocking collectives, traded(): return lax.all_to_all(blocks, axes, split_axis=0, concat_axis=0, tiled=True)  115 us
    ppermute x12, waiting for transfers between devices, gathered(): lax.ppermute(block, axes, [(i, (i + k) % count) for i in range(count)])  36.1 us
    pallas_call x10, Pallas kernels, call(): pl.pallas_call(kernel, out_shape=out_shapes, in_specs=in_specs, out_specs...  17.2 us
    ppermute x1, waiting for transfers between devices, body(): lax.ppermute(lax.dynamic_slice_in_dim(value, far, 16, 0), 'zl', swap)  16.6 us
    all_to_all x3, starting transfers between devices, traded(): return lax.all_to_all(blocks, axes, split_axis=0, concat_axis=0, tiled=True)  13.6 us
    ppermute x1, waiting for transfers between devices, body(): lax.ppermute(lax.dynamic_slice_in_dim(key, far, 16, 0), 'zl', swap)  11.2 us
    all_to_all x3, waiting for transfers between devices, traded(): return lax.all_to_all(blocks, axes, split_axis=0, concat_axis=0, tiled=True)  10.9 us
    ppermute x12, starting transfers between devices, gathered(): lax.ppermute(block, axes, [(i, (i + k) % count) for i in range(count)])  9.56 us
  transfers between devices with their start and end apart: 18, of which 16 were waited for; matrix products, arithmetic and copies ran while one was open for 1% of the time, Pallas kernels for 0%

profile of v1, /device:TPU:1, one launch (start us, length us, event | category | flops | bytes accessed | tf_op | source)
XLA Modules:
  0.0 251.3 jit_solution(1721327719133506493)
XLA Ops:
  1.5 20.9 %all_to_all.50 = bf16[8,32,2048]{2,1,0:T(8,128)(2,1)S(1)} all-to-all(bf16[8,32,2048]{2,1,0:T(8,128)(2,1)S(1)} %bitcast.60), channel_id=1, replica_groups=mesh['s'=2,'x'=4,'c'=2,'y'=4,'zh'=2,'zl'=2] {'x','c'}, dimensions={0} | all-to-all | bytes 2097152 | tf_op jit(solution)/shard_map/all_to_all | solution.py:43
  25.4 5.0 %all-to-all-start.1 = ((bf16[16,16,1152]{2,1,0:T(8,128)(2,1)}), bf16[16,16,1152]{2,1,0:T(8,128)(2,1)}, u32[]{:S(2)}, u32[]{:S(2)}) async-start(bf16[16,16,1152]{2,1,0:T(8,128)(2,1)} %bitcast.56), calls=%async_computation.1 | async-start | bytes 1179648 | tf_op jit(solution)/shard_map/all_to_all | solution.py:43
  33.8 16.6 %collective-permute-done.1.value_other_ref = bf16[16,64,256]{2,1,0:T(8,128)(2,1)} collective-permute-done((bf16[16,64,256]{2,1,0:T(8,128)(2,1)}, bf16[16,64,256]{2,1,0:T(8,128)(2,1)}, u32[]{:S(2)}, u32[]{:S(2)}) %collective-permute-start.1) | collective-permute-done | bytes 524320 | tf_op jit(solution)/shard_map/ppermute | solution.py:237
  50.4 11.2 %collective-permute-done.key_other_ref = bf16[16,64,256]{2,1,0:T(8,128)(2,1)} collective-permute-done((bf16[16,64,256]{2,1,0:T(8,128)(2,1)}, bf16[16,64,256]{2,1,0:T(8,128)(2,1)}, u32[]{:S(2)}, u32[]{:S(2)}) %collective-permute-start) | collective-permute-done | bytes 524320 | tf_op jit(solution)/shard_map/ppermute | solution.py:236
  61.6 3.3 %attend.2 = bf16[16,16,1024]{2,1,0:T(8,128)(2,1)S(1)} custom-call(s32[3]{0:T(128)S(1)} %pad_add_fusion.place_ref, bf16[16,16,1152]{2,1,0:T(8,128)(2,1)} %all-to-all-done.1.sums_ref, s32[256,1]{1,0:T(8,128)S(1)} %broadcast_in_dim_tile.4.live_ref, bf16[32,64,256]{2,1,0:T(8,128)(2,1)S(1)} %bitcast.47, bf16[16,64,256]{2,1,0:T(8,128)(2,1)} %collective-permute-done.key_other_ref, ...), custom_call_target="tpu_custom_call" | custom-call | flops 536870912 | bytes 4260876 | tf_op jit(solution)/shard_map/attend/pallas_call | solution.py:23
  65.0 14.6 %all_to_all.51 = bf16[16,16,1024]{2,1,0:T(8,128)(2,1)S(1)} all-to-all(bf16[16,16,1024]{2,1,0:T(8,128)(2,1)S(1)} %attend.2), channel_id=1, replica_groups=mesh['s'=2,'x'=4,'c'=2,'y'=4,'zh'=2,'zl'=2] {'x','c','zl'}, dimensions={0} | all-to-all | bytes 1048576 | tf_op jit(solution)/shard_map/all_to_all | solution.py:43
  82.1 18.2 %all_to_all.52.blocks_ref = bf16[4,4,256,128]{3,2,1,0:T(8,128)(2,1)S(1)} all-to-all(bf16[4,4,256,128]{3,2,1,0:T(8,128)(2,1)S(1)} %bitcast.53), channel_id=1, replica_groups=mesh['s'=2,'x'=4,'c'=2,'y'=4,'zh'=2,'zl'=2] {'y'}, dimensions={0} | all-to-all | bytes 2097152 | tf_op jit(solution)/shard_map/all_to_all | solution.py:43
  101.2 5.1 %all-to-all-start.4 = ((bf16[4,256,128]{2,1,0:T(8,128)(2,1)}), bf16[4,256,128]{2,1,0:T(8,128)(2,1)S(1)}, u32[]{:S(2)}, u32[]{:S(2)}) async-start(bf16[4,256,128]{2,1,0:T(8,128)(2,1)} %merge.2), calls=%async_computation.4 | async-start | bytes 524288 | tf_op jit(solution)/shard_map/all_to_all | solution.py:43
  107.0 5.0 %all-to-all-done.4.blocks_ref = bf16[4,256,128]{2,1,0:T(8,128)(2,1)S(1)} async-done(((bf16[4,256,128]{2,1,0:T(8,128)(2,1)}), bf16[4,256,128]{2,1,0:T(8,128)(2,1)S(1)}, u32[]{:S(2)}, u32[]{:S(2)}) %all-to-all-start.4) | async-done | bytes 262176 | tf_op jit(solution)/shard_map/all_to_all | solution.py:43
  112.9 7.1 %collective-permute-start.2 = (bf16[256,128]{1,0:T(8,128)(2,1)S(1)}, bf16[256,128]{1,0:T(8,128)(2,1)S(1)}, u32[]{:S(2)}, u32[]{:S(2)}) collective-permute-start(bf16[256,128]{1,0:T(8,128)(2,1)S(1)} %merge_state.2), channel_id=1, source_target_pairs={{0,128},{1,129},{2,130},{3,131},{4,132},{5,133},{6,134},{7,135},{8... | collective-permute-start | bytes 196616 | tf_op jit(solution)/shard_map/ppermute | solution.py:254
  121.3 3.5 %collective-permute-start.5 = (bf16[256,128]{1,0:T(8,128)(2,1)S(1)}, bf16[256,128]{1,0:T(8,128)(2,1)S(1)}, u32[]{:S(2)}, u32[]{:S(2)}) collective-permute-start(bf16[256,128]{1,0:T(8,128)(2,1)S(1)} %collective-permute-done.2.state_ref), channel_id=1, source_target_pairs={{0,3},{1,0},{2,1},{3,2},{4,7},{5,4},{6,5},{7,6},{8,11},{9,8},{10,9... | collective-permute-start | bytes 196616 | tf_op jit(solution)/shard_map/ppermute | solution.py:37
  132.6 3.1 %collective-permute-done.8.three_ref = bf16[4,256,128]{2,1,0:T(8,128)(2,1)S(1)} collective-permute-done((bf16[4,256,128]{2,1,0:T(8,128)(2,1)S(1)}, bf16[4,256,128]{2,1,0:T(8,128)(2,1)S(1)}, u32[]{:S(2)}, u32[]{:S(2)}) %collective-permute-start.8) | collective-permute-done | bytes 262176 | tf_op jit(solution)/shard_map/ppermute | solution.py:37
  138.3 3.6 %collective-permute-done.6.one_ref = bf16[4,256,128]{2,1,0:T(8,128)(2,1)S(1)} collective-permute-done((bf16[4,256,128]{2,1,0:T(8,128)(2,1)S(1)}, bf16[4,256,128]{2,1,0:T(8,128)(2,1)S(1)}, u32[]{:S(2)}, u32[]{:S(2)}) %collective-permute-start.6) | collective-permute-done | bytes 262176 | tf_op jit(solution)/shard_map/ppermute | solution.py:37
  144.1 3.0 %project_chunks.1 = bf16[256,1152]{1,0:T(8,128)(2,1)S(1)} custom-call(s32[3]{0:T(128)S(1)} %pad_add_fusion.place_ref, bf16[4,256,128]{2,1,0:T(8,128)(2,1)S(1)} %pad_maximum_fusion.own_ref, bf16[4,256,128]{2,1,0:T(8,128)(2,1)S(1)} %collective-permute-done.6.one_ref, bf16[4,256,128]{2,1,0:T(8,128)(2,1)S(1)} %collective-permute-done.7.two_ref, ...), custom_call_target="tpu_custom_call" | custom-call | flops 1073741824 | bytes 6291456 | tf_op jit(solution)/shard_map/project_chunks/pallas_call | solution.py:256
  147.1 20.1 %all_to_all.53.sums_ref = bf16[16,16,1152]{2,1,0:T(8,128)(2,1)S(1)} all-to-all(bf16[16,16,1152]{2,1,0:T(8,128)(2,1)S(1)} %bitcast.55), channel_id=1, replica_groups=mesh['s'=2,'x'=4,'c'=2,'y'=4,'zh'=2,'zl'=2] {'x','c','zl'}, dimensions={0} | all-to-all | bytes 1179648 | tf_op jit(solution)/shard_map/all_to_all | solution.py:43
  167.1 3.0 %attend.3 = bf16[16,16,1024]{2,1,0:T(8,128)(2,1)S(1)} custom-call(s32[3]{0:T(128)S(1)} %pad_add_fusion.place_ref, bf16[16,16,1152]{2,1,0:T(8,128)(2,1)S(1)} %all_to_all.53.sums_ref, s32[256,1]{1,0:T(8,128)S(1)} %broadcast_in_dim_tile.4.live_ref, bf16[32,64,256]{2,1,0:T(8,128)(2,1)S(1)} %bitcast.48, bf16[16,64,256]{2,1,0:T(8,128)(2,1)} %collective-permute-done.key_other_ref, ...), custom_call_target="tpu_custom_call" | custom-call | flops 536870912 | bytes 4260876 | tf_op jit(solution)/shard_map/attend/pallas_call | solution.py:23
  170.2 12.5 %all_to_all.54 = bf16[16,16,1024]{2,1,0:T(8,128)(2,1)S(1)} all-to-all(bf16[16,16,1024]{2,1,0:T(8,128)(2,1)S(1)} %attend.3), channel_id=1, replica_groups=mesh['s'=2,'x'=4,'c'=2,'y'=4,'zh'=2,'zl'=2] {'x','c','zl'}, dimensions={0} | all-to-all | bytes 1048576 | tf_op jit(solution)/shard_map/all_to_all | solution.py:43
  185.2 17.2 %all_to_all.55.blocks_ref = bf16[4,4,256,128]{3,2,1,0:T(8,128)(2,1)S(1)} all-to-all(bf16[4,4,256,128]{3,2,1,0:T(8,128)(2,1)S(1)} %bitcast.54), channel_id=1, replica_groups=mesh['s'=2,'x'=4,'c'=2,'y'=4,'zh'=2,'zl'=2] {'y'}, dimensions={0} | all-to-all | bytes 2097152 | tf_op jit(solution)/shard_map/all_to_all | solution.py:43
  203.3 3.4 %all-to-all-start.8 = ((bf16[4,256,128]{2,1,0:T(8,128)(2,1)}), bf16[4,256,128]{2,1,0:T(8,128)(2,1)S(1)}, u32[]{:S(2)}, u32[]{:S(2)}) async-start(bf16[4,256,128]{2,1,0:T(8,128)(2,1)} %merge.3), calls=%async_computation.8 | async-start | bytes 524288 | tf_op jit(solution)/shard_map/all_to_all | solution.py:43
  206.7 5.9 %all-to-all-done.8.blocks_ref = bf16[4,256,128]{2,1,0:T(8,128)(2,1)S(1)} async-done(((bf16[4,256,128]{2,1,0:T(8,128)(2,1)}), bf16[4,256,128]{2,1,0:T(8,128)(2,1)S(1)}, u32[]{:S(2)}, u32[]{:S(2)}) %all-to-all-start.8) | async-done | bytes 262176 | tf_op jit(solution)/shard_map/all_to_all | solution.py:43
  212.6 11.6 %all_to_all.56 = bf16[8,32,128]{2,1,0:T(8,128)(2,1)S(1)} all-to-all(bf16[8,32,128]{2,1,0:T(8,128)(2,1)S(1)} %bitcast.62), channel_id=1, replica_groups=mesh['s'=2,'x'=4,'c'=2,'y'=4,'zh'=2,'zl'=2] {'x','c'}, dimensions={0} | all-to-all | bytes 131072 | tf_op jit(solution)/shard_map/all_to_all | solution.py:43
  227.3 5.7 %collective-permute-done.10 = bf16[8,32,128]{2,1,0:T(8,128)(2,1)S(1)} collective-permute-done((bf16[8,32,128]{2,1,0:T(8,128)(2,1)S(1)}, bf16[8,32,128]{2,1,0:T(8,128)(2,1)S(1)}, u32[]{:S(2)}, u32[]{:S(2)}) %collective-permute-start.10) | collective-permute-done | bytes 65568 | tf_op jit(solution)/shard_map/ppermute | solution.py:37
  235.2 5.2 %collective-permute-done.14.three_ref = bf16[4,8,32,128]{3,2,1,0:T(8,128)(2,1)S(1)} collective-permute-done((bf16[4,8,32,128]{3,2,1,0:T(8,128)(2,1)S(1)}, bf16[4,8,32,128]{3,2,1,0:T(8,128)(2,1)S(1)}, u32[]{:S(2)}, u32[]{:S(2)}) %collective-permute-start.14) | collective-permute-done | bytes 262176 | tf_op jit(solution)/shard_map/ppermute | solution.py:37
  242.5 6.9 %collective-permute-done.12.one_ref = bf16[4,8,32,128]{3,2,1,0:T(8,128)(2,1)S(1)} collective-permute-done((bf16[4,8,32,128]{3,2,1,0:T(8,128)(2,1)S(1)}, bf16[4,8,32,128]{3,2,1,0:T(8,128)(2,1)S(1)}, u32[]{:S(2)}, u32[]{:S(2)}) %collective-permute-start.12) | collective-permute-done | bytes 262176 | tf_op jit(solution)/shard_map/ppermute | solution.py:37
  (59 shorter events, 39.4 us)
Async XLA Ops:
  0.0 22.3 %copy-start = (bf16[1,2048,1024]{2,1,0:T(8,128)(2,1)S(1)}, bf16[1,2048,1024]{2,1,0:T(8,128)(2,1)}, u32[]{:S(2)}) copy-start(bf16[1,2048,1024]{2,1,0:T(8,128)(2,1)} %param.7) | copy-start | bytes 12582916
  1.5 28.9 %copy-start.5 = (bf16[1,32,256,64]{2,3,1,0:T(8,128)(2,1)S(1)}, bf16[1,32,256,64]{2,3,1,0:T(8,128)(2,1)}, u32[]{:S(2)}) copy-start(bf16[1,32,256,64]{2,3,1,0:T(8,128)(2,1)} %param.10) | copy-start | bytes 3145732
  22.3 10.3 %copy-start.4 = (bf16[1,32,256,64]{2,3,1,0:T(8,128)(2,1)S(1)}, bf16[1,32,256,64]{2,3,1,0:T(8,128)(2,1)}, u32[]{:S(2)}) copy-start(bf16[1,32,256,64]{2,3,1,0:T(8,128)(2,1)} %param.9) | copy-start | bytes 3145732
  22.4 11.2 %copy-start.8 = (s32[32]{0:T(128)S(1)}, s32[32]{0:T(128)}, u32[]{:S(2)}) copy-start(s32[32]{0:T(128)} %param.11) | copy-start | bytes 388
  25.4 36.3 %all-to-all-start.1 = ((bf16[16,16,1152]{2,1,0:T(8,128)(2,1)}), bf16[16,16,1152]{2,1,0:T(8,128)(2,1)}, u32[]{:S(2)}, u32[]{:S(2)}) async-start(bf16[16,16,1152]{2,1,0:T(8,128)(2,1)} %bitcast.56), calls=%async_computation.1 | async-start | bytes 1179648 | tf_op jit(solution)/shard_map/all_to_all | solution.py:43
  31.2 19.2 %collective-permute-start.1 = (bf16[16,64,256]{2,1,0:T(8,128)(2,1)}, bf16[16,64,256]{2,1,0:T(8,128)(2,1)}, u32[]{:S(2)}, u32[]{:S(2)}) collective-permute-start(bf16[16,64,256]{2,1,0:T(8,128)(2,1)} %dynamic-slice_bitcast_fusion), channel_id=1, source_target_pairs={{0,1},{1,0},{2,3},{3,2},{4,5},{5,4},{6,7},{7,6},{8,9},{9,8},{10,11... | collective-permute-start | bytes 1572872 | tf_op jit(solution)/shard_map/ppermute | solution.py:237
  33.5 28.2 %collective-permute-start = (bf16[16,64,256]{2,1,0:T(8,128)(2,1)}, bf16[16,64,256]{2,1,0:T(8,128)(2,1)}, u32[]{:S(2)}, u32[]{:S(2)}) collective-permute-start(bf16[16,64,256]{2,1,0:T(8,128)(2,1)} %dynamic-slice_bitcast_fusion.1), channel_id=1, source_target_pairs={{0,1},{1,0},{2,3},{3,2},{4,5},{5,4},{6,7},{7,6},{8,9},{9,8},{10,11... | collective-permute-start | bytes 1572872 | tf_op jit(solution)/shard_map/ppermute | solution.py:236
  61.6 18.0 %copy-start.2 = (bf16[1,1024,2048]{2,1,0:T(8,128)(2,1)S(1)}, bf16[1,1024,2048]{2,1,0:T(8,128)(2,1)}, u32[]{:S(2)}) copy-start(bf16[1,1024,2048]{2,1,0:T(8,128)(2,1)} %param.8) | copy-start | bytes 12582916
  101.2 10.8 %all-to-all-start.4 = ((bf16[4,256,128]{2,1,0:T(8,128)(2,1)}), bf16[4,256,128]{2,1,0:T(8,128)(2,1)S(1)}, u32[]{:S(2)}, u32[]{:S(2)}) async-start(bf16[4,256,128]{2,1,0:T(8,128)(2,1)} %merge.2), calls=%async_computation.4 | async-start | bytes 524288 | tf_op jit(solution)/shard_map/all_to_all | solution.py:43
  112.9 8.4 %collective-permute-start.2 = (bf16[256,128]{1,0:T(8,128)(2,1)S(1)}, bf16[256,128]{1,0:T(8,128)(2,1)S(1)}, u32[]{:S(2)}, u32[]{:S(2)}) collective-permute-start(bf16[256,128]{1,0:T(8,128)(2,1)S(1)} %merge_state.2), channel_id=1, source_target_pairs={{0,128},{1,129},{2,130},{3,131},{4,132},{5,133},{6,134},{7,135},{8... | collective-permute-start | bytes 196616 | tf_op jit(solution)/shard_map/ppermute | solution.py:254
  121.3 5.4 %collective-permute-start.5 = (bf16[256,128]{1,0:T(8,128)(2,1)S(1)}, bf16[256,128]{1,0:T(8,128)(2,1)S(1)}, u32[]{:S(2)}, u32[]{:S(2)}) collective-permute-start(bf16[256,128]{1,0:T(8,128)(2,1)S(1)} %collective-permute-done.2.state_ref), channel_id=1, source_target_pairs={{0,3},{1,0},{2,1},{3,2},{4,7},{5,4},{6,5},{7,6},{8,11},{9,8},{10,9... | collective-permute-start | bytes 196616 | tf_op jit(solution)/shard_map/ppermute | solution.py:37
  124.8 4.0 %collective-permute-start.4 = (bf16[256,128]{1,0:T(8,128)(2,1)S(1)}, bf16[256,128]{1,0:T(8,128)(2,1)S(1)}, u32[]{:S(2)}, u32[]{:S(2)}) collective-permute-start(bf16[256,128]{1,0:T(8,128)(2,1)S(1)} %collective-permute-done.2.state_ref), channel_id=1, source_target_pairs={{0,2},{1,3},{2,0},{3,1},{4,6},{5,7},{6,4},{7,5},{8,10},{9,11},{10,... | collective-permute-start | bytes 196616 | tf_op jit(solution)/shard_map/ppermute | solution.py:37
  124.8 5.6 %collective-permute-start.3 = (bf16[256,128]{1,0:T(8,128)(2,1)S(1)}, bf16[256,128]{1,0:T(8,128)(2,1)S(1)}, u32[]{:S(2)}, u32[]{:S(2)}) collective-permute-start(bf16[256,128]{1,0:T(8,128)(2,1)S(1)} %collective-permute-done.2.state_ref), channel_id=1, source_target_pairs={{0,1},{1,2},{2,3},{3,0},{4,5},{5,6},{6,7},{7,4},{8,9},{9,10},{10,1... | collective-permute-start | bytes 196616 | tf_op jit(solution)/shard_map/ppermute | solution.py:37
  130.5 5.3 %collective-permute-start.8 = (bf16[4,256,128]{2,1,0:T(8,128)(2,1)S(1)}, bf16[4,256,128]{2,1,0:T(8,128)(2,1)S(1)}, u32[]{:S(2)}, u32[]{:S(2)}) collective-permute-start(bf16[4,256,128]{2,1,0:T(8,128)(2,1)S(1)} %pad_maximum_fusion.own_ref), channel_id=1, source_target_pairs={{0,12},{4,0},{8,4},{12,8},{1,13},{5,1},{9,5},{13,9},{2,14},{6,2},{... | collective-permute-start | bytes 786440 | tf_op jit(solution)/shard_map/ppermute | solution.py:37
  131.4 6.8 %collective-permute-start.7 = (bf16[4,256,128]{2,1,0:T(8,128)(2,1)S(1)}, bf16[4,256,128]{2,1,0:T(8,128)(2,1)S(1)}, u32[]{:S(2)}, u32[]{:S(2)}) collective-permute-start(bf16[4,256,128]{2,1,0:T(8,128)(2,1)S(1)} %pad_maximum_fusion.own_ref), channel_id=1, source_target_pairs={{0,8},{4,12},{8,0},{12,4},{1,9},{5,13},{9,1},{13,5},{2,10},{6,14},... | collective-permute-start | bytes 786440 | tf_op jit(solution)/shard_map/ppermute | solution.py:37
  132.6 9.2 %collective-permute-start.6 = (bf16[4,256,128]{2,1,0:T(8,128)(2,1)S(1)}, bf16[4,256,128]{2,1,0:T(8,128)(2,1)S(1)}, u32[]{:S(2)}, u32[]{:S(2)}) collective-permute-start(bf16[4,256,128]{2,1,0:T(8,128)(2,1)S(1)} %pad_maximum_fusion.own_ref), channel_id=1, source_target_pairs={{0,4},{4,8},{8,12},{12,0},{1,5},{5,9},{9,13},{13,1},{2,6},{6,10},{... | collective-permute-start | bytes 786440 | tf_op jit(solution)/shard_map/ppermute | solution.py:37
  147.1 35.7 %copy-start.3 = (bf16[1,1024,2048]{2,1,0:T(8,128)(2,1)S(1)}, bf16[1,1024,2048]{2,1,0:T(8,128)(2,1)}, u32[]{:S(2)}) copy-start(bf16[1,1024,2048]{2,1,0:T(8,128)(2,1)} %param.8) | copy-start | bytes 12582916
  203.3 9.3 %all-to-all-start.8 = ((bf16[4,256,128]{2,1,0:T(8,128)(2,1)}), bf16[4,256,128]{2,1,0:T(8,128)(2,1)S(1)}, u32[]{:S(2)}, u32[]{:S(2)}) async-start(bf16[4,256,128]{2,1,0:T(8,128)(2,1)} %merge.3), calls=%async_computation.8 | async-start | bytes 524288 | tf_op jit(solution)/shard_map/all_to_all | solution.py:43
  224.2 3.1 %collective-permute-start.11 = (bf16[8,32,128]{2,1,0:T(8,128)(2,1)S(1)}, bf16[8,32,128]{2,1,0:T(8,128)(2,1)S(1)}, u32[]{:S(2)}, u32[]{:S(2)}) collective-permute-start(bf16[8,32,128]{2,1,0:T(8,128)(2,1)S(1)} %all_to_all.56), channel_id=1, source_target_pairs={{0,3},{1,0},{2,1},{3,2},{4,7},{5,4},{6,5},{7,6},{8,11},{9,8},{10,9... | collective-permute-start | bytes 196616 | tf_op jit(solution)/shard_map/ppermute | solution.py:37
  225.4 7.6 %collective-permute-start.10 = (bf16[8,32,128]{2,1,0:T(8,128)(2,1)S(1)}, bf16[8,32,128]{2,1,0:T(8,128)(2,1)S(1)}, u32[]{:S(2)}, u32[]{:S(2)}) collective-permute-start(bf16[8,32,128]{2,1,0:T(8,128)(2,1)S(1)} %all_to_all.56), channel_id=1, source_target_pairs={{0,2},{1,3},{2,0},{3,1},{4,6},{5,7},{6,4},{7,5},{8,10},{9,11},{10,... | collective-permute-start | bytes 196616 | tf_op jit(solution)/shard_map/ppermute | solution.py:37
  225.4 7.6 %collective-permute-start.9 = (bf16[8,32,128]{2,1,0:T(8,128)(2,1)S(1)}, bf16[8,32,128]{2,1,0:T(8,128)(2,1)S(1)}, u32[]{:S(2)}, u32[]{:S(2)}) collective-permute-start(bf16[8,32,128]{2,1,0:T(8,128)(2,1)S(1)} %all_to_all.56), channel_id=1, source_target_pairs={{0,1},{1,2},{2,3},{3,0},{4,5},{5,6},{6,7},{7,4},{8,9},{9,10},{10,1... | collective-permute-start | bytes 196616 | tf_op jit(solution)/shard_map/ppermute | solution.py:37
  233.1 7.3 %collective-permute-start.14 = (bf16[4,8,32,128]{3,2,1,0:T(8,128)(2,1)S(1)}, bf16[4,8,32,128]{3,2,1,0:T(8,128)(2,1)S(1)}, u32[]{:S(2)}, u32[]{:S(2)}) collective-permute-start(bf16[4,8,32,128]{3,2,1,0:T(8,128)(2,1)S(1)} %pad_maximum_fusion.1.own_ref), channel_id=1, source_target_pairs={{0,12},{4,0},{8,4},{12,8},{1,13},{5,1},{9,5},{13,9},{2,14},{6,2},{... | collective-permute-start | bytes 786440 | tf_op jit(solution)/shard_map/ppermute | solution.py:37
  234.0 8.5 %collective-permute-start.13 = (bf16[4,8,32,128]{3,2,1,0:T(8,128)(2,1)S(1)}, bf16[4,8,32,128]{3,2,1,0:T(8,128)(2,1)S(1)}, u32[]{:S(2)}, u32[]{:S(2)}) collective-permute-start(bf16[4,8,32,128]{3,2,1,0:T(8,128)(2,1)S(1)} %pad_maximum_fusion.1.own_ref), channel_id=1, source_target_pairs={{0,8},{4,12},{8,0},{12,4},{1,9},{5,13},{9,1},{13,5},{2,10},{6,14},... | collective-permute-start | bytes 786440 | tf_op jit(solution)/shard_map/ppermute | solution.py:37
  235.2 14.2 %collective-permute-start.12 = (bf16[4,8,32,128]{3,2,1,0:T(8,128)(2,1)S(1)}, bf16[4,8,32,128]{3,2,1,0:T(8,128)(2,1)S(1)}, u32[]{:S(2)}, u32[]{:S(2)}) collective-permute-start(bf16[4,8,32,128]{3,2,1,0:T(8,128)(2,1)S(1)} %pad_maximum_fusion.1.own_ref), channel_id=1, source_target_pairs={{0,4},{4,8},{8,12},{12,0},{1,5},{5,9},{9,13},{13,1},{2,6},{6,10},{... | collective-permute-start | bytes 786440 | tf_op jit(solution)/shard_map/ppermute | solution.py:37
  (3 other events, 3.8 us)
